TPU v7x, 32 devices: a whole 2x2x4 slice. The times are simulated.
32 devices in a mesh: parts: 2 (over x), cand: 16 (over z, y, core).
Axes of the slice: x: 2, y: 2, z: 4, core: 2. Of those that a mesh axis runs over, the one named last changes fastest.
Arguments:
- user_rows: bfloat16 [128, 16, 128], P(('parts', 'cand')), parts along dimension 0, may hold values from -6 to 6
- item_table: bfloat16 [8192, 512], P(('parts', 'cand')), parts along dimension 0, may hold values from -6 to 6
- cand_request: int32 [65536], P(('parts', 'cand')), parts along dimension 0, may hold values from 0 to 63, never falling along the last dimension, each value on 1 to 1000 neighbouring positions
- request_order: int32 [128], P('parts'), parts along dimension 0, may hold values from 0 to 63, as said below
- item_shard: int32 [65536, 1], P(('parts', 'cand')), parts along dimension 0, may hold values from 0 to 15; in each aligned block of 2048 rows (0 to 2047, 2048 to 4095, ...) at most 256 rows name the same one
- item_offset: int32 [65536], P(('parts', 'cand')), parts along dimension 0, may hold values from 0 to 255
- w_user: bfloat16 [256, 2048], replicated, may hold values from -0.375 to 0.375
- w_dots: bfloat16 [64, 2048], replicated, may hold values from -0.75 to 0.75
- w_item_gram: bfloat16 [16, 2048], replicated, may hold values from -1.5 to 1.5
- w_item: bfloat16 [512, 2048], replicated, may hold values from -0.25 to 0.25
- bias_one: bfloat16 [2048], replicated, may hold values from -3 to 3
- w_out: bfloat16 [2048], replicated, may hold values from -0.125 to 0.125
Outputs:
- scores: float32 [65536], P(('parts', 'cand')), parts along dimension 0
There are 2 independent parts, one for each index of `parts`. A program takes and returns all parts, laid end to end along the dimension named above; an argument that names none is the same for every part. Nothing has to cross between parts.
Inputs may be any that keep to these rules, and one draw needn't show every extreme that they name: `cand_request`: never falls; each segment has 1 to 1000 candidates, one exactly 1000. `request_order`: a permutation of the requests. `item_shard`: among the candidates of one device at most 256 name one shard; some shard is named exactly 256 times by some device.
All inputs are finite; a program needn't handle non-finite values.
Results may differ from a plain program's by a relative error of at most 0.0035.
Values may be sent and summed in bfloat16 or wider, within the bound.
A program may use at most 128 MiB of HBM per device.

v0:
```python
import math

import jax
import jax.numpy as jnp
from jax import lax
from jax.sharding import PartitionSpec as P


def shards(
    user_rows,
    item_table,
    cand_request,
    request_order,
    item_shard,
    item_offset,
    w_user,
    w_dots,
    w_item_gram,
    w_item,
    bias_one,
    w_out,
):
    req_dev, user_feats, feat_width = user_rows.shape
    cand_dev = cand_request.shape[0]
    item_dev, row_width = item_table.shape
    item_feats = row_width // feat_width
    num_cand = lax.axis_size("cand")
    flat_users = user_rows.reshape(req_dev, user_feats * feat_width)
    user_gram = (
        jnp.einsum("rue,rve->ruv", user_rows, user_rows, preferred_element_type=jnp.float32)
        / feat_width
    ).astype(jnp.bfloat16)
    user_gram = user_gram.reshape(req_dev, user_feats * user_feats)
    cand_req = jnp.take(request_order, cand_request, axis=0)
    own_term = jnp.dot(user_gram, w_user, preferred_element_type=jnp.float32).astype(jnp.bfloat16)
    all_users, all_terms = (
        lax.all_gather(flat_users, "cand", axis=0, tiled=True),
        lax.all_gather(own_term, "cand", axis=0, tiled=True),
    )
    picked_users = jnp.take(all_users, cand_req, axis=0).reshape(cand_dev, user_feats, feat_width)
    picked_term = jnp.take(all_terms, cand_req, axis=0)
    src_shard = item_shard[:, 0]
    most_slots = 2 * cand_dev // num_cand
    shard_hits = (src_shard[:, None] == jnp.arange(num_cand, dtype=jnp.int32)[None, :]).astype(
        jnp.int32
    )
    slot_index = jnp.sum((jnp.cumsum(shard_hits, axis=0) - shard_hits) * shard_hits, axis=1)
    asked = jnp.zeros((num_cand, most_slots), jnp.int32).at[src_shard, slot_index].set(item_offset)
    found = jnp.take(
        item_table, lax.all_to_all(asked, "cand", split_axis=0, concat_axis=0, tiled=True), axis=0
    )
    fetched = lax.all_to_all(found, "cand", split_axis=0, concat_axis=0, tiled=True)
    items = fetched[src_shard, slot_index]
    items_three = items.reshape(cand_dev, item_feats, feat_width)
    dots = (
        jnp.einsum("cue,cie->cui", picked_users, items_three, preferred_element_type=jnp.float32)
        / math.sqrt(feat_width)
    ).astype(jnp.bfloat16)
    dots = dots.reshape(cand_dev, user_feats * item_feats)
    item_gram = (
        jnp.einsum("cie,cje->cij", items_three, items_three, preferred_element_type=jnp.float32)
        / feat_width
    ).astype(jnp.bfloat16)
    item_gram = item_gram.reshape(cand_dev, item_feats * item_feats)
    preact = picked_term.astype(jnp.float32) + jnp.dot(
        dots, w_dots, preferred_element_type=jnp.float32
    )
    preact = preact + jnp.dot(item_gram, w_item_gram, preferred_element_type=jnp.float32)
    preact = preact + jnp.dot(items, w_item, preferred_element_type=jnp.float32)
    preact = preact + bias_one.astype(jnp.float32)
    hidden = jax.nn.relu(preact).astype(jnp.bfloat16)
    return jnp.dot(hidden, w_out, preferred_element_type=jnp.float32)


def solution(mesh):
    in_specs = (
        P(("parts", "cand"), None, None),
        P(("parts", "cand"), None),
        P(("parts", "cand")),
        P("parts"),
        P(("parts", "cand"), None),
        P(("parts", "cand")),
        P(),
        P(),
        P(),
        P(),
        P(),
        P(),
    )
    out_specs = P(("parts", "cand"))
    return jax.shard_map(shards, mesh=mesh, in_specs=in_specs, out_specs=out_specs, check_vma=False)
```

profile of v0, /device:TPU:0, one launch (start us, length us, event | category | flops | bytes accessed | tf_op | source)
XLA Modules:
  0.0 363.0 jit_solution(5302436270684198041)
XLA Ops:
  0.0 0.9 fusion.6
  0.9 4.5 %reduce-window.6 = s32[16,16,128]{2,1,0:T(8,128)S(1)} reduce-window(s32[16,16,128]{2,1,0:T(8,128)S(1)} %fusion.6, s32[]{:T(128)} %constant.37.clone.1), window={size=1x1x128 pad=0_0x0_0x127_0}, to_apply=%region_0.0 | reduce-window | flops 4161536 | bytes 262148 | tf_op jit(solution)/shard_map/reduce-window
  5.4 0.4 slice_reduce_fusion
  5.9 0.2 reduce-window.9
  6.0 0.1 broadcast_add_fusion
  6.1 0.8 fusion.5
  6.9 0.7 shift-left_or_fusion
  7.6 0.8 and_reduce_fusion
  8.4 0.7 multiply_reduce_fusion
  9.2 8.2 %scatter_custom_fusion = s32[4096]{0:T(1024)S(1)} fusion(s32[2048]{0:T(1024)S(1)} %broadcast_select_fusion.1, s32[2048]{0:T(1024)} %param.19, s32[]{:T(128)} %constant.37.clone.1), kind=kCustom, calls=%fused_computation.37 | custom fusion | bytes 16896
  17.4 13.7 %all_to_all.20 = s32[16,1,256]{2,1,0:T(1,128)S(1)} all-to-all(s32[16,1,256]{2,1,0:T(1,128)S(1)} %bitcast.127), channel_id=1, replica_groups=mesh['parts'=2,'cand'=16] {'cand'}, dimensions={0} | all-to-all | bytes 32768 | tf_op jit(solution)/shard_map/all_to_all | solution.py:50
  31.1 17.3 %gather_fusion = bf16[4096,512]{1,0:T(8,128)(2,1)} fusion(bf16[256,512]{1,0:T(8,128)(2,1)S(1)} %copy-done.1, s32[4096]{0:T(1024)S(1)} %broadcast_clamp_fusion), kind=kCustom, calls=%fused_computation.2 | custom fusion | bytes 8404992 | tf_op jit(solution)/shard_map/jit(_take)/gather | solution.py:49
  48.4 0.0 copy-start.7
  48.4 0.0 copy-start.8
  48.4 0.0 copy-start.4
  48.5 0.0 copy-start.2
  48.5 0.0 copy-start.6
  48.5 3.9 %broadcast_select_fusion = bf16[16,256,512]{2,1,0:T(8,128)(2,1)} fusion(bf16[16,256,512]{2,1,0:T(8,128)(2,1)} %bitcast.123, pred[16,256]{1,0:T(8,128)(4,1)S(1)} %compare_and_fusion), kind=kLoop, calls=%fused_computation.7 | loop fusion | flops 2097152 | bytes 8392704 | tf_op jit(solution)/shard_map/jit(_take)/select_n | solution.py:49
  52.4 4.5 %all-to-all-start.1 = ((bf16[16,256,512]{2,1,0:T(8,128)(2,1)}), bf16[16,256,512]{2,1,0:T(8,128)(2,1)}, u32[]{:S(2)}, u32[]{:S(2)}) async-start(bf16[16,256,512]{2,1,0:T(8,128)(2,1)} %broadcast_select_fusion), calls=%async_computation.1 | async-start | bytes 8388608 | tf_op jit(solution)/shard_map/all_to_all | solution.py:52
  57.0 0.1 fusion.2
  57.1 0.1 reshape.94
  57.2 1.5 fusion.1
  58.7 86.2 %all-gather = bf16[16,4,2048]{2,1,0:T(4,128)(2,1)S(1)} all-gather(bf16[1,4,2048]{2,1,0:T(4,128)(2,1)S(1)} %fusion.1), channel_id=1, replica_groups=mesh['parts'=2,'cand'=16] {'cand'}, dimensions={0}, use_global_device_ids=true | all-gather | bytes 278528 | tf_op jit(solution)/shard_map/all_gather | solution.py:38
  145.0 0.1 reshape.218
  145.0 35.8 %all-gather.1 = bf16[16,4,2048]{2,1,0:T(4,128)(2,1)S(1)} all-gather(bf16[1,4,2048]{2,1,0:T(4,128)(2,1)S(1)} %reshape.219), channel_id=1, replica_groups=mesh['parts'=2,'cand'=16] {'cand'}, dimensions={0}, use_global_device_ids=true | all-gather | bytes 278528 | tf_op jit(solution)/shard_map/all_gather | solution.py:37
  180.8 0.1 reshape.220
  180.9 0.7 fusion.14
  181.6 0.7 fusion.13
  182.3 0.7 fusion.12
  183.0 0.7 fusion.11
  183.8 39.9 %compare_and_fusion.1 = (pred[2048]{0:T(1024)(128)(4,1)S(1)}, s32[2048]{0:T(1024)S(1)}) fusion(s32[]{:T(128)} %bitcast.63, s32[]{:T(128)} %bitcast.62, s32[]{:T(128)} %bitcast.61, s32[]{:T(128)} %bitcast.60, s32[]{:T(128)} %bitcast.59, s32[]{:T(128)} %bitcast.58, s32[]{:T(128)} %bitcast.57, s32[]{:T(128)} %bitcast.56, s32[]{:T(128)} %bitcast.55, ...), kind=kLoop, calls=%fused_computation.39 | loop fusion | flops 284672 | bytes 18688 | tf_op jit(solution)/shard_map/jit(_take)/and | solution.py:41
  223.7 11.2 %gather_fusion.3 = bf16[2048,2048]{1,0:T(8,128)(2,1)} fusion(bf16[64,2048]{1,0:T(8,128)(2,1)S(1)} %reshape.220, s32[2048]{0:T(1024)S(1)} %broadcast_clamp_fusion.1), kind=kCustom, calls=%fused_computation.1.clone | custom fusion | bytes 16785408 | tf_op jit(solution)/shard_map/jit(_take)/gather | solution.py:40
  234.9 7.4 %select_bitcast_fusion = bf16[256,8,16,128]{3,1,2,0:T(8,128)(2,1)} fusion(bf16[2048,2048]{1,0:T(8,128)(2,1)} %gather_fusion.3, pred[2048]{0:T(1024)(128)(4,1)S(1)} %get-tuple-element.6), kind=kLoop, calls=%fused_computation.6 | loop fusion | flops 4194304 | bytes 16779264
  242.3 9.8 %copy.21 = bf16[256,8,16,128]{3,2,1,0:T(8,128)(2,1)} copy(bf16[256,8,16,128]{3,1,2,0:T(8,128)(2,1)} %select_bitcast_fusion) | data formatting | bytes 16777216
  252.0 10.9 %gather_fusion.2 = bf16[2048,2048]{1,0:T(8,128)(2,1)} fusion(bf16[64,2048]{1,0:T(8,128)(2,1)S(1)} %reshape.218, s32[2048]{0:T(1024)S(1)} %broadcast_clamp_fusion.1), kind=kCustom, calls=%fused_computation.clone | custom fusion | bytes 16785408 | tf_op jit(solution)/shard_map/jit(_take)/gather | solution.py:41
  263.0 0.0 all-to-all-done.1
  263.0 37.0 %gather_fusion.1 = bf16[2048,512]{1,0:T(8,128)(2,1)} fusion(bf16[16,256,512]{2,1,0:T(8,128)(2,1)} %all-to-all-done.1, s32[2048]{0:T(1024)S(1)} %bitcast.121), kind=kCustom, calls=%fused_computation.3 | custom fusion | bytes 4210688 | tf_op jit(solution)/shard_map/gather | solution.py:53
  300.0 4.0 %reshape.98 = bf16[2048,4,128]{2,1,0:T(4,128)(2,1)} reshape(bf16[2048,512]{1,0:T(8,128)(2,1)} %gather_fusion.1) | data formatting | bytes 4194304 | tf_op jit(solution)/shard_map/reshape | solution.py:54
  304.0 6.5 %fusion.16 = f32[2048,4,4]{2,1,0:T(4,128)} fusion(bf16[2048,4,128]{2,1,0:T(4,128)(2,1)} %reshape.98), kind=kOutput, calls=%fused_computation.49 | convolution fusion | flops 8388608 | bytes 2228224 | tf_op jit(solution)/shard_map/cie,cje->cij/dot_general | solution.py:61
  310.5 3.5 copy.19
  314.1 10.4 %fusion.15 = f32[2048,16,4]{1,2,0:T(4,128)} fusion(bf16[2048,16,128]{2,1,0:T(8,128)(2,1)} %bitcast.122, bf16[2048,4,128]{2,1,0:T(4,128)(2,1)} %reshape.98), kind=kOutput, calls=%fused_computation.48 | convolution fusion | flops 33554432 | bytes 11010048 | tf_op jit(solution)/shard_map/cue,cie->cui/dot_general | solution.py:56
  324.5 3.4 copy.17
  328.0 0.2 copy.18
  328.2 0.1 reshape.99
  328.3 0.0 copy-start.5
  328.3 9.9 %fusion.18 = f32[2048,2048]{1,0:T(8,128)} fusion(bf16[2048,512]{1,0:T(8,128)(2,1)} %gather_fusion.1, bf16[512,2048]{1,0:T(8,128)(2,1)S(1)} %copy-done), kind=kOutput, calls=%fused_computation.51 | convolution fusion | flops 4294967296 | bytes 20971520 | tf_op jit(solution)/shard_map/dot_general | solution.py:69
  338.2 8.1 %fusion.17 = f32[2048,2048]{1,0:T(8,128)} fusion(bf16[2048,16]{0,1:T(8,128)(2,1)S(1)} %reshape.100, bf16[16,2048]{1,0:T(8,128)(2,1)S(1)} %copy-done.5), kind=kOutput, calls=%fused_computation.50 | convolution fusion | flops 134217728 | bytes 16908288 | tf_op jit(solution)/shard_map/dot_general | solution.py:68
  346.3 16.7 %fusion = f32[1,2048]{1,0:T(1,128)} fusion(bf16[2048,1]{0,1:T(2,128)(2,1)S(1)} %reshape.226, f32[2048,2048]{1,0:T(8,128)} %fusion.18, f32[2048,2048]{1,0:T(8,128)} %fusion.17, bf16[2048,64]{0,1:T(8,128)(2,1)S(1)} %reshape.99, bf16[64,2048]{1,0:T(8,128)(2,1)S(1)} %copy-done.3, bf16[2048,2048]{1,0:T(8,128)(2,1)} %gather_fusion.2, ...), kind=kOutput, calls=%fused_computation.8 | convolution fusion | flops 578813952 | bytes 42489856 | tf_op jit(solution)/shard_map/dot_general | solution.py:72
  (23 shorter events, 0.2 us)
Async XLA Ops:
  0.0 328.3 %copy-start = (bf16[512,2048]{1,0:T(8,128)(2,1)S(1)}, bf16[512,2048]{1,0:T(8,128)(2,1)}, u32[]{:S(2)}) copy-start(bf16[512,2048]{1,0:T(8,128)(2,1)} %param.23) | copy-start | bytes 6291460
  0.0 31.1 %copy-start.1 = (bf16[256,512]{1,0:T(8,128)(2,1)S(1)}, bf16[256,512]{1,0:T(8,128)(2,1)}, u32[]{:S(2)}) copy-start(bf16[256,512]{1,0:T(8,128)(2,1)} %param.15) | copy-start | bytes 786436
  48.4 8.5 %copy-start.7 = (bf16[2048]{0:T(1024)(128)(2,1)S(1)}, bf16[2048]{0:T(1024)(128)(2,1)}, u32[]{:S(2)}) copy-start(bf16[2048]{0:T(1024)(128)(2,1)} %param.24) | copy-start | bytes 12292
  48.4 8.5 %copy-start.8 = (bf16[2048]{0:T(1024)(128)(2,1)S(1)}, bf16[2048]{0:T(1024)(128)(2,1)}, u32[]{:S(2)}) copy-start(bf16[2048]{0:T(1024)(128)(2,1)} %param.25) | copy-start | bytes 12292
  48.4 8.6 %copy-start.4 = (bf16[4,16,128]{2,1,0:T(8,128)(2,1)S(1)}, bf16[4,16,128]{2,1,0:T(8,128)(2,1)}, u32[]{:S(2)}) copy-start(bf16[4,16,128]{2,1,0:T(8,128)(2,1)} %param.14) | copy-start | bytes 49156
  48.5 132.4 %copy-start.2 = (s32[64]{0:T(128)S(1)}, s32[64]{0:T(128)}, u32[]{:S(2)}) copy-start(s32[64]{0:T(128)} %param.17) | copy-start | bytes 772
  48.5 135.3 %copy-start.6 = (s32[2048]{0:T(1024)S(1)}, s32[2048]{0:T(1024)}, u32[]{:S(2)}) copy-start(s32[2048]{0:T(1024)} %param.16) | copy-start | bytes 24580
  52.4 210.6 %all-to-all-start.1 = ((bf16[16,256,512]{2,1,0:T(8,128)(2,1)}), bf16[16,256,512]{2,1,0:T(8,128)(2,1)}, u32[]{:S(2)}, u32[]{:S(2)}) async-start(bf16[16,256,512]{2,1,0:T(8,128)(2,1)} %broadcast_select_fusion), calls=%async_computation.1 | async-start | bytes 8388608 | tf_op jit(solution)/shard_map/all_to_all | solution.py:52
  328.3 9.9 %copy-start.5 = (bf16[16,2048]{1,0:T(8,128)(2,1)S(1)}, bf16[16,2048]{1,0:T(8,128)(2,1)}, u32[]{:S(2)}) copy-start(bf16[16,2048]{1,0:T(8,128)(2,1)} %param.22) | copy-start | bytes 196612
  338.2 8.1 %copy-start.3 = (bf16[64,2048]{1,0:T(8,128)(2,1)S(1)}, bf16[64,2048]{1,0:T(8,128)(2,1)}, u32[]{:S(2)}) copy-start(bf16[64,2048]{1,0:T(8,128)(2,1)} %param.21) | copy-start | bytes 786436
where the time goes:
time: 365 us; the launch traced here: 363 us
  blocking collectives  136 us (37%)
  local copies, waits for them, and re-layouts  109 us (30%)
  other arithmetic  60.1 us (16%)
  matrix products  53.2 us (15%)
  starting transfers between devices  4.54 us (1%)
    all_gather x1, blocking collectives, shards(): lax.all_gather(own_term, 'cand', axis=0, tiled=True)  86.2 us
    and x1, other arithmetic, shards(): picked_term = jnp.take(all_terms, cand_req, axis=0)  39.9 us
    gather x1, local copies, waits for them, and re-layouts, shards(): items = fetched[src_shard, slot_index]  37 us
    all_gather x1, blocking collectives, shards(): lax.all_gather(flat_users, 'cand', axis=0, tiled=True)  35.8 us
    unnamed x24, local copies, waits for them, and re-layouts  18.2 us
    gather x1, local copies, waits for them, and re-layouts, shards(): jnp.take(item_table, lax.all_to_all(asked, 'cand', split_axis=0, concat_a...  17.3 us
    dot_general x1, matrix products, shards(): return jnp.dot(hidden, w_out, preferred_element_type=jnp.float32)  16.7 us
    all_to_all x1, blocking collectives, shards(): lax.all_to_all(asked, 'cand', split_axis=0, concat_axis=0, tiled=True)  13.7 us
  transfers between devices with their start and end apart: 1, of which 0 were waited for; matrix products, arithmetic and copies ran while one was open for 23% of the time, Pallas kernels for 0%

commit v1 on v0

v1 whole, which is shorter than its diff:
```python
import functools
import math

import jax
import jax.numpy as jnp
from jax import lax
from jax.experimental import pallas as pl
from jax.experimental.pallas import tpu as pltpu
from jax.sharding import PartitionSpec as P

BF16 = jnp.bfloat16
F32 = jnp.float32
I32 = jnp.int32


def iota(shape, dim):
    return lax.broadcasted_iota(I32, shape, dim)


def onehot(mask):
    return jnp.where(mask, F32(1), F32(0)).astype(BF16)


def kernel(
    dims,
    users_hbm,
    table_hbm,
    seg_ref,
    order_ref,
    shard_ref,
    offset_ref,
    w_user_hbm,
    w_dots_ref,
    w_gram_ref,
    w_item_hbm,
    bias_ref,
    w_out_ref,
    out_ref,
    buf,
    xt,
    wt,
    wut,
    w_item,
    w_user,
    w_tail,
    tt,
    users,
    gram_t,
    wout_b,
    rid,
    req,
    load_sem,
    send_sem,
    recv_sem,
):
    nz, ny, req_dev, feats, width, nif, item_dev, cands, hidden = dims
    nreq = nz * ny * 2 * req_dev
    row = nif * width
    per_slot = req_dev * feats
    piece = per_slot // nif
    shift = feats.bit_length() - 1
    me = lax.axis_index("cand")
    core = me % 2
    y = (me // 2) % ny
    z = me // (2 * ny)

    def index(zz, yy, cc):
        return (zz * ny + yy) * 2 + cc

    up, down = index(z + 1, y, core), index(z - 1, y, core)
    across, beside = index(z, ny - 1 - y, core), index(z, y, 1 - core)

    loads = []
    for i in range(nif):
        loads.append(
            pltpu.make_async_copy(
                table_hbm.at[:, pl.ds(i * width, width)],
                buf.at[me, i, pl.ds(0, item_dev)],
                load_sem.at[2 * i],
            )
        )
        loads.append(
            pltpu.make_async_copy(
                users_hbm.at[pl.ds(i * piece, piece)],
                buf.at[me, i, pl.ds(item_dev, piece)],
                load_sem.at[2 * i + 1],
            )
        )
    for load in loads:
        load.start()
    get_item = pltpu.make_async_copy(w_item_hbm, w_item, load_sem.at[2 * nif])
    get_user = pltpu.make_async_copy(w_user_hbm, w_user, load_sem.at[2 * nif + 1])
    get_item.start()
    get_user.start()

    barrier = pltpu.get_barrier_semaphore()

    def near(device, exists):
        @pl.when(exists)
        def _():
            pl.semaphore_signal(
                barrier, inc=1, device_id={"cand": device}, device_id_type=pl.DeviceIdType.MESH
            )

    always = z >= 0
    near(up, z + 1 < nz)
    near(down, z > 0)
    if ny == 2:
        near(across, always)
    near(beside, always)
    peers = ny + (z + 1 < nz).astype(I32) + (z > 0).astype(I32)
    pl.semaphore_wait(barrier, peers)

    def copy(slot, way, device):
        return pltpu.make_async_remote_copy(
            src_ref=buf.at[slot],
            dst_ref=buf.at[slot],
            send_sem=send_sem.at[way, slot],
            recv_sem=recv_sem.at[slot],
            device_id={"cand": device},
            device_id_type=pl.DeviceIdType.MESH,
        )

    def await_slot(slot):
        copy(slot, 0, beside).wait_recv()

    for load in loads:
        load.wait()

    @pl.when(z + 1 < nz)
    def _():
        copy(me, 0, up).start()

    @pl.when(z > 0)
    def _():
        copy(me, 1, down).start()

    if ny == 2:
        copy(me, 2, across).start()
    copy(me, 3, beside).start()

    xt[...] = jnp.zeros_like(xt)
    gram_t[...] = jnp.zeros_like(gram_t)
    rid[...] = shard_ref[...] * item_dev + offset_ref[...]
    seg = seg_ref[...]
    req[...] = lax.fori_loop(
        0,
        nreq,
        lambda s, total: total + jnp.where(seg == s, order_ref[s], 0),
        jnp.zeros_like(seg),
    )
    nd, ng = feats * nif, nif * nif
    turn = onehot(
        iota((nd, nd), 1) == (iota((nd, nd), 0) & (feats - 1)) * nif + (iota((nd, nd), 0) >> shift)
    )
    w_tail[...] = jnp.zeros_like(w_tail)
    w_tail[0:nd] = jnp.dot(turn, w_dots_ref[...], preferred_element_type=F32).astype(BF16)
    w_tail[nd : nd + ng] = w_gram_ref[...]
    bias_row = jnp.broadcast_to(bias_ref[...].astype(F32), (16, hidden))
    w_tail[nd + ng : nd + ng + 16] = jnp.where(iota((16, hidden), 0) == 0, bias_row, 0.0).astype(
        BF16
    )
    base = w_tail.shape[0]
    step_h = 256

    get_item.wait()
    get_user.wait()

    @pl.loop(0, hidden // step_h)
    def _(h):
        at = pl.ds(pl.multiple_of(h * step_h, step_h), step_h)
        wt[at, 0:row] = w_item[:, at].T
        wt[at, row : row + base] = w_tail[:, at].T
        wut[at, :] = w_user[:, at].T
        wout_b[at, :] = jnp.broadcast_to(w_out_ref[:, at].astype(F32), (128, step_h)).T

    pair_rows = 2 * item_dev
    block = 512
    nu = 2 * per_slot
    nf = feats * feats

    def take_in(zz, yy, exists):
        @pl.when(exists)
        def _():
            first = index(zz, yy, 0)
            await_slot(first + 1 - core)
            for lane in range(2):
                for i in range(nif):
                    tt[i * width : (i + 1) * width, lane * item_dev : (lane + 1) * item_dev] = buf[
                        first + lane, i, 0:item_dev, :
                    ].T

            @pl.loop(0, cands // block)
            def _(n):
                at = pl.ds(pl.multiple_of(n * block, block), block)
                hit = onehot(rid[:, at] - first * item_dev == iota((pair_rows, block), 0))
                xt[0:row, at] += jnp.dot(tt[...], hit, preferred_element_type=F32).astype(BF16)

            here = buf[pl.ds(first, 2), :, item_dev : item_dev + piece, :].reshape(nu, width)
            users[pl.ds(pl.multiple_of(first * per_slot, nu), nu), :] = here
            gram = lax.dot_general(
                here, here, (((1,), (1,)), ((), ())), preferred_element_type=F32
            ) * F32(1 / width)
            same = (iota((nu, nu), 0) >> shift) == (iota((nu, nu), 1) >> shift)
            gram = jnp.where(same, gram, 0.0).astype(BF16)
            spread = onehot((iota((nf, nu), 0) >> shift) == (iota((nf, nu), 1) & (feats - 1)))
            wide = jnp.dot(spread, gram, preferred_element_type=F32)
            keep = (iota((nf, nu), 0) & (feats - 1)) == (iota((nf, nu), 1) & (feats - 1))
            wide = jnp.where(keep, wide, 0.0).astype(BF16)
            place = onehot(
                iota((nu, nreq), 1) == first * req_dev + (iota((nu, nreq), 0) >> shift)
            )
            gram_t[...] += jnp.dot(wide, place, preferred_element_type=F32)

    @pl.loop(1, nz + 2)
    def _(t):
        later = t < nz
        low, high = z - t, z + t

        @pl.when(later & (low >= 0))
        def _():
            slot = index(low, y, core)
            await_slot(slot)

            @pl.when(z + 1 < nz)
            def _():
                copy(slot, 0, up).start()

            if ny == 2:
                copy(slot, 2, across).start()
            copy(slot, 3, beside).start()

        @pl.when(later & (high < nz))
        def _():
            slot = index(high, y, core)
            await_slot(slot)

            @pl.when(z > 0)
            def _():
                copy(slot, 1, down).start()

            if ny == 2:
                copy(slot, 2, across).start()
            copy(slot, 3, beside).start()

        a, b = z - (t - 1), z + (t - 1)
        has_a, has_b = (a >= 0) & (t <= nz), (b < nz) & (t >= 2) & (t <= nz)
        if ny == 2:
            for zz, has in ((a, has_a), (b, has_b)):

                @pl.when(has)
                def _(zz=zz):
                    slot = index(zz, 1 - y, core)
                    await_slot(slot)
                    copy(slot, 3, beside).start()

        take_in(a, y, has_a)
        take_in(b, y, has_b)
        if ny == 2:
            c, d = z - (t - 2), z + (t - 2)
            take_in(c, 1 - y, (c >= 0) & (t >= 2))
            take_in(d, 1 - y, (d < nz) & (t >= 3))

    term_at = row + base

    @pl.loop(0, hidden // step_h)
    def _(h):
        at = pl.ds(pl.multiple_of(h * step_h, step_h), step_h)
        wt[at, term_at : term_at + nreq] = jnp.dot(
            wut[at, :], gram_t[...].astype(BF16), preferred_element_type=F32
        ).astype(BF16)

    span = 256

    @pl.loop(0, cands // span)
    def _(n):
        at = pl.ds(pl.multiple_of(n * span, span), span)
        who = req[:, at]
        group = 16
        vectors = []
        for i in range(nif):
            item = xt[i * width : (i + 1) * width, at]
            total = jnp.zeros((feats, span), F32)
            for g in range(nreq // group):
                rows = group * feats
                z_all = jnp.dot(
                    users[g * rows : (g + 1) * rows, :], item, preferred_element_type=F32
                ).reshape(group, feats, span)
                hit = (who == iota((group, span), 0) + g * group)[:, None, :]
                total = total + jnp.sum(jnp.where(hit, z_all, 0.0), axis=0)
            xt[row + i * feats : row + (i + 1) * feats, at] = (
                total * F32(1 / math.sqrt(width))
            ).astype(BF16)
            vectors.append(item.astype(F32))
        grams = {}
        for i in range(nif):
            for j in range(i, nif):
                grams[i, j] = grams[j, i] = jnp.sum(
                    vectors[i] * vectors[j], axis=0, keepdims=True
                )
        gram_rows = jnp.concatenate(
            [grams[i, j] for i in range(nif) for j in range(nif)], axis=0
        ) * F32(1 / width)
        xt[row + nd : row + nd + ng, at] = gram_rows.astype(BF16)
        xt[row + nd + ng : row + nd + ng + 16, at] = onehot(iota((16, span), 0) == 0)
        xt[term_at : term_at + nreq, at] = onehot(who == iota((nreq, span), 0))
        x = xt[:, at]
        score = jnp.zeros((8, span), F32)
        for h in range(hidden // step_h):
            pre = jnp.dot(
                wt[h * step_h : (h + 1) * step_h, :], x, preferred_element_type=F32
            )
            w = wout_b[h * step_h : (h + 1) * step_h, :]
            act = jnp.maximum(pre, 0.0) * jnp.concatenate([w] * (span // 128), axis=1)
            score = score + jnp.sum(act.reshape(step_h // 8, 8, span), axis=0)
        out_ref[:, at] = jnp.sum(score, axis=0, keepdims=True)

    @pl.when(z + 1 < nz)
    def _():
        @pl.loop(0, nz)
        def _(zz):
            @pl.when(zz <= z)
            def _():
                copy(index(zz, y, core), 0, up).wait_send()

    @pl.when(z > 0)
    def _():
        @pl.loop(0, nz)
        def _(zz):
            @pl.when(zz >= z)
            def _():
                copy(index(zz, y, core), 1, down).wait_send()

    @pl.loop(0, nz)
    def _(zz):
        if ny == 2:
            copy(index(zz, y, core), 2, across).wait_send()
        for yy in range(ny):
            copy(index(zz, yy, core), 3, beside).wait_send()


def shards(
    ny,
    user_rows,
    item_table,
    cand_request,
    request_order,
    item_shard,
    item_offset,
    w_user,
    w_dots,
    w_item_gram,
    w_item,
    bias_one,
    w_out,
):
    req_dev, feats, width = user_rows.shape
    item_dev, row = item_table.shape
    nif = row // width
    cands = cand_request.shape[0]
    hidden = w_out.shape[0]
    num = lax.axis_size("cand")
    nz = num // (2 * ny)
    nreq = num * req_dev
    base = -(-(feats * nif + nif * nif + 16) // 128) * 128
    depth = row + base + -(-nreq // 128) * 128
    slot_rows = item_dev + req_dev * feats // nif
    vmem = pl.BlockSpec(memory_space=pltpu.VMEM)
    smem = pl.BlockSpec(memory_space=pltpu.SMEM)
    hbm = pl.BlockSpec(memory_space=pl.ANY)
    dims = (nz, ny, req_dev, feats, width, nif, item_dev, cands, hidden)
    scores = pl.pallas_call(
        functools.partial(kernel, dims),
        out_shape=jax.ShapeDtypeStruct((1, cands), F32),
        in_specs=[hbm, hbm, vmem, smem, vmem, vmem, hbm, vmem, vmem, hbm, vmem, vmem],
        out_specs=vmem,
        scratch_shapes=[
            pltpu.VMEM((num, nif, slot_rows, width), BF16),
            pltpu.VMEM((depth, cands), BF16),
            pltpu.VMEM((hidden, depth), BF16),
            pltpu.VMEM((hidden, feats * feats), BF16),
            pltpu.VMEM((row, hidden), BF16),
            pltpu.VMEM((feats * feats, hidden), BF16),
            pltpu.VMEM((base, hidden), BF16),
            pltpu.VMEM((row, 2 * item_dev), BF16),
            pltpu.VMEM((nreq * feats, width), BF16),
            pltpu.VMEM((feats * feats, nreq), F32),
            pltpu.VMEM((hidden, 128), F32),
            pltpu.VMEM((1, cands), I32),
            pltpu.VMEM((1, cands), I32),
            pltpu.SemaphoreType.DMA((2 * nif + 2,)),
            pltpu.SemaphoreType.DMA((4, num)),
            pltpu.SemaphoreType.DMA((num,)),
        ],
        compiler_params=pltpu.CompilerParams(
            collective_id=0, has_side_effects=True, vmem_limit_bytes=56 * 1024 * 1024
        ),
        cost_estimate=pl.CostEstimate(
            flops=2 * cands * hidden * depth, bytes_accessed=8 << 20, transcendentals=0
        ),
    )(
        user_rows.reshape(req_dev * feats, width),
        item_table,
        cand_request.reshape(1, cands),
        request_order,
        item_shard.reshape(1, cands),
        item_offset.reshape(1, cands),
        w_user,
        w_dots,
        w_item_gram,
        w_item,
        bias_one.reshape(1, hidden),
        w_out.reshape(1, hidden),
    )
    return scores.reshape(cands)


def solution(mesh):
    ny = 4 // mesh.shape["parts"]
    in_specs = (
        P(("parts", "cand"), None, None),
        P(("parts", "cand"), None),
        P(("parts", "cand")),
        P("parts"),
        P(("parts", "cand"), None),
        P(("parts", "cand")),
        P(),
        P(),
        P(),
        P(),
        P(),
        P(),
    )
    out_specs = P(("parts", "cand"))
    return jax.shard_map(
        functools.partial(shards, ny),
        mesh=mesh,
        in_specs=in_specs,
        out_specs=out_specs,
        check_vma=False,
    )
```

time: 365 us -> 61.6 us (0.17)
  the two profiles are of different devices: /device:TPU:0 before, /device:TPU:8 now
where the time goes in v1:
time: 61.6 us; the launch traced here: 61.3 us
  Pallas kernels  57.4 us (93%)
  local copies, waits for them, and re-layouts  3.87 us (6%)
    pallas_call x1, Pallas kernels, shards(): pl.pallas_call(functools.partial(kernel, dims), out_shape=jax.ShapeDtypeS...  57.4 us
    unnamed x1, local copies, waits for them, and re-layouts  1.3 us
    reshape x1, local copies, waits for them, and re-layouts, shards(): bias_one.reshape(1, hidden)  1.29 us
    reshape x1, local copies, waits for them, and re-layouts, shards(): w_out.reshape(1, hidden)  1.29 us

profile of v1, /device:TPU:8, one launch (start us, length us, event | category | flops | bytes accessed | tf_op | source)
XLA Modules:
  0.0 61.3 jit_solution(14683753174147570159)
XLA Ops:
  0.0 1.3 %reshape.25.bias_ref = bf16[1,2048]{1,0:T(2,128)(2,1)} reshape(bf16[2048]{0:T(1024)(128)(2,1)} %param.22) | data formatting | bytes 8192 | tf_op jit(solution)/shard_map/reshape | solution.py:412
  1.3 1.3 %reshape.26.w_out_ref = bf16[1,2048]{1,0:T(2,128)(2,1)} reshape(bf16[2048]{0:T(1024)(128)(2,1)} %param.23) | data formatting | bytes 8192 | tf_op jit(solution)/shard_map/reshape | solution.py:413
  2.6 57.4 %shard_map.118 = f32[1,2048]{1,0:T(1,128)} custom-call(bf16[64,128]{1,0:T(8,128)(2,1)} %bitcast.6, bf16[256,512]{1,0:T(8,128)(2,1)} %table_hbm.1, s32[1,2048]{1,0:T(1,128)} %bitcast.7, s32[64]{0:T(128)} %order_ref.1, s32[1,2048]{1,0:T(1,128)} %bitcast.8, s32[1,2048]{1,0:T(1,128)} %bitcast.9, bf16[256,2048]{1,0:T(8,128)(2,1)} %w_user_hbm.1, ...), custom_call_target="tpu_custom_call" | custom-call | flops 6442450944 | bytes 8388608 | tf_op jit(solution)/shard_map/pallas_call | solution.py:372
  60.0 1.3 %copy.14 = f32[2048]{0:T(1024)} copy(f32[2048]{0:T(1024)} %bitcast.5) | data formatting | bytes 16384

commit v2 on v1

--- a/solution.py
+++ b/solution.py
@@ -111,33 +111,63 @@
     peers = ny + (z + 1 < nz).astype(I32) + (z > 0).astype(I32)
     pl.semaphore_wait(barrier, peers)
 
-    def copy(slot, way, device):
+    balanced = ny == 2 and nz >= 4
+    part = nif // 2
+
+    def copy(slot, half, way, device):
         return pltpu.make_async_remote_copy(
-            src_ref=buf.at[slot],
-            dst_ref=buf.at[slot],
-            send_sem=send_sem.at[way, slot],
-            recv_sem=recv_sem.at[slot],
+            src_ref=buf.at[slot, pl.ds(half * part, part)],
+            dst_ref=buf.at[slot, pl.ds(half * part, part)],
+            send_sem=send_sem.at[way, slot, half],
+            recv_sem=recv_sem.at[slot, half],
             device_id={"cand": device},
             device_id_type=pl.DeviceIdType.MESH,
         )
 
-    def await_slot(slot):
-        copy(slot, 0, beside).wait_recv()
+    def await_half(slot, half):
+        copy(slot, half, 0, beside).wait_recv()
+
+    def forward(zz, own_column, half, act):
+        slot = index(zz, y if own_column else 1 - y, core)
+        if own_column:
+            go_up, go_down, go_across = zz <= z, zz >= z, None
+            if balanced:
+                by_z = ((z == 1) & (zz == 0)) | ((z == nz - 2) & (zz == nz - 1))
+                if half == 1:
+                    by_z |= ((z == 0) & (zz == nz - 1)) | ((z == nz - 1) & (zz == 0))
+                go_across = jnp.logical_not(by_z)
+            elif ny == 2:
+                go_across = always
+        else:
+            go_up = go_down = go_across = None
+            if balanced:
+                go_up, go_down = (z == 0) & (zz == 0), (z == nz - 1) & (zz == nz - 1)
+                if half == 1:
+                    go_up |= (z == nz - 2) & (zz == 0)
+                    go_down |= (z == 1) & (zz == nz - 1)
+        for way, device, go in (
+            (0, up, None if go_up is None else go_up & (z + 1 < nz)),
+            (1, down, None if go_down is None else go_down & (z > 0)),
+            (2, across, go_across),
+            (3, beside, always),
+        ):
+            if go is not None:
+
+                @pl.when(go)
+                def _(way=way, device=device):
+                    act(copy(slot, half, way, device))
+
+    def start(c):
+        c.start()
+
+    def finish(c):
+        c.wait_send()
 
     for load in loads:
         load.wait()
 
-    @pl.when(z + 1 < nz)
-    def _():
-        copy(me, 0, up).start()
-
-    @pl.when(z > 0)
-    def _():
-        copy(me, 1, down).start()
-
-    if ny == 2:
-        copy(me, 2, across).start()
-    copy(me, 3, beside).start()
+    for half in range(2):
+        forward(z, True, half, start)
 
     xt[...] = jnp.zeros_like(xt)
     gram_t[...] = jnp.zeros_like(gram_t)
@@ -156,7 +186,7 @@
     w_tail[...] = jnp.zeros_like(w_tail)
     w_tail[0:nd] = jnp.dot(turn, w_dots_ref[...], preferred_element_type=F32).astype(BF16)
     w_tail[nd : nd + ng] = w_gram_ref[...]
-    bias_row = jnp.broadcast_to(bias_ref[...].astype(F32), (16, hidden))
+    bias_row = jnp.broadcast_to(bias_ref[...].astype(F32).reshape(1, hidden), (16, hidden))
     w_tail[nd + ng : nd + ng + 16] = jnp.where(iota((16, hidden), 0) == 0, bias_row, 0.0).astype(
         BF16
     )
@@ -172,7 +202,7 @@
         wt[at, 0:row] = w_item[:, at].T
         wt[at, row : row + base] = w_tail[:, at].T
         wut[at, :] = w_user[:, at].T
-        wout_b[at, :] = jnp.broadcast_to(w_out_ref[:, at].astype(F32), (128, step_h)).T
+        wout_b[at, :] = jnp.broadcast_to(w_out_ref[at].astype(F32).reshape(1, step_h), (128, step_h)).T
 
     pair_rows = 2 * item_dev
     block = 512
@@ -183,18 +213,19 @@
         @pl.when(exists)
         def _():
             first = index(zz, yy, 0)
-            await_slot(first + 1 - core)
+            for half in range(2):
+                await_half(first + 1 - core, half)
             for lane in range(2):
                 for i in range(nif):
                     tt[i * width : (i + 1) * width, lane * item_dev : (lane + 1) * item_dev] = buf[
                         first + lane, i, 0:item_dev, :
                     ].T
 
-            @pl.loop(0, cands // block)
-            def _(n):
-                at = pl.ds(pl.multiple_of(n * block, block), block)
+            rows_t = tt[...]
+            for n in range(cands // block):
+                at = pl.ds(n * block, block)
                 hit = onehot(rid[:, at] - first * item_dev == iota((pair_rows, block), 0))
-                xt[0:row, at] += jnp.dot(tt[...], hit, preferred_element_type=F32).astype(BF16)
+                xt[0:row, at] += jnp.dot(rows_t, hit, preferred_element_type=F32).astype(BF16)
 
             here = buf[pl.ds(first, 2), :, item_dev : item_dev + piece, :].reshape(nu, width)
             users[pl.ds(pl.multiple_of(first * per_slot, nu), nu), :] = here
@@ -212,54 +243,29 @@
             )
             gram_t[...] += jnp.dot(wide, place, preferred_element_type=F32)
 
+    def relay(zz, own_column, half, exists):
+        @pl.when(exists)
+        def _():
+            await_half(index(zz, y if own_column else 1 - y, core), half)
+            forward(zz, own_column, half, start)
+
     @pl.loop(1, nz + 2)
     def _(t):
-        later = t < nz
-        low, high = z - t, z + t
-
-        @pl.when(later & (low >= 0))
-        def _():
-            slot = index(low, y, core)
-            await_slot(slot)
-
-            @pl.when(z + 1 < nz)
-            def _():
-                copy(slot, 0, up).start()
-
-            if ny == 2:
-                copy(slot, 2, across).start()
-            copy(slot, 3, beside).start()
-
-        @pl.when(later & (high < nz))
-        def _():
-            slot = index(high, y, core)
-            await_slot(slot)
-
-            @pl.when(z > 0)
-            def _():
-                copy(slot, 1, down).start()
-
-            if ny == 2:
-                copy(slot, 2, across).start()
-            copy(slot, 3, beside).start()
-
         a, b = z - (t - 1), z + (t - 1)
         has_a, has_b = (a >= 0) & (t <= nz), (b < nz) & (t >= 2) & (t <= nz)
-        if ny == 2:
-            for zz, has in ((a, has_a), (b, has_b)):
-
-                @pl.when(has)
-                def _(zz=zz):
-                    slot = index(zz, 1 - y, core)
-                    await_slot(slot)
-                    copy(slot, 3, beside).start()
-
-        take_in(a, y, has_a)
-        take_in(b, y, has_b)
-        if ny == 2:
-            c, d = z - (t - 2), z + (t - 2)
-            take_in(c, 1 - y, (c >= 0) & (t >= 2))
-            take_in(d, 1 - y, (d < nz) & (t >= 3))
+        c, d = z - (t - 2), z + (t - 2)
+        for half in range(2):
+            relay(z - t, True, half, (t < nz) & (z - t >= 0))
+            relay(z + t, True, half, (t < nz) & (z + t < nz))
+            if ny == 2:
+                relay(a, False, half, has_a)
+                relay(b, False, half, has_b)
+            if half == 0:
+                take_in(a, y, has_a)
+                take_in(b, y, has_b)
+            elif ny == 2:
+                take_in(c, 1 - y, (c >= 0) & (t >= 2))
+                take_in(d, 1 - y, (d < nz) & (t >= 3))
 
     term_at = row + base
 
@@ -272,7 +278,7 @@
 
     span = 256
 
-    @pl.loop(0, cands // span)
+    @pl.loop(0, cands // span, unroll=2)
     def _(n):
         at = pl.ds(pl.multiple_of(n * span, span), span)
         who = req[:, at]
@@ -315,28 +321,12 @@
             score = score + jnp.sum(act.reshape(step_h // 8, 8, span), axis=0)
         out_ref[:, at] = jnp.sum(score, axis=0, keepdims=True)
 
-    @pl.when(z + 1 < nz)
-    def _():
-        @pl.loop(0, nz)
-        def _(zz):
-            @pl.when(zz <= z)
-            def _():
-                copy(index(zz, y, core), 0, up).wait_send()
-
-    @pl.when(z > 0)
-    def _():
-        @pl.loop(0, nz)
-        def _(zz):
-            @pl.when(zz >= z)
-            def _():
-                copy(index(zz, y, core), 1, down).wait_send()
-
     @pl.loop(0, nz)
     def _(zz):
-        if ny == 2:
-            copy(index(zz, y, core), 2, across).wait_send()
-        for yy in range(ny):
-            copy(index(zz, yy, core), 3, beside).wait_send()
+        for half in range(2):
+            forward(zz, True, half, finish)
+            if ny == 2:
+                forward(zz, False, half, finish)
 
 
 def shards(
@@ -389,8 +379,8 @@
             pltpu.VMEM((1, cands), I32),
             pltpu.VMEM((1, cands), I32),
             pltpu.SemaphoreType.DMA((2 * nif + 2,)),
-            pltpu.SemaphoreType.DMA((4, num)),
-            pltpu.SemaphoreType.DMA((num,)),
+            pltpu.SemaphoreType.DMA((4, num, 2)),
+            pltpu.SemaphoreType.DMA((num, 2)),
         ],
         compiler_params=pltpu.CompilerParams(
             collective_id=0, has_side_effects=True, vmem_limit_bytes=56 * 1024 * 1024
@@ -409,8 +399,8 @@
         w_dots,
         w_item_gram,
         w_item,
-        bias_one.reshape(1, hidden),
-        w_out.reshape(1, hidden),
+        bias_one,
+        w_out,
     )
     return scores.reshape(cands)
 

time: 61.6 us -> 49.9 us (0.81)
  the two profiles are of different devices: /device:TPU:8 before, /device:TPU:0 now
where the time goes in v2:
time: 49.9 us; the launch traced here: 49.7 us
  Pallas kernels  48.4 us (97%)
  local copies, waits for them, and re-layouts  1.3 us (3%)
    pallas_call x1, Pallas kernels, shards(): pl.pallas_call(functools.partial(kernel, dims), out_shape=jax.ShapeDtypeS...  48.4 us
    unnamed x1, local copies, waits for them, and re-layouts  1.3 us

profile of v2, /device:TPU:0, one launch (start us, length us, event | category | flops | bytes accessed | tf_op | source)
XLA Modules:
  0.0 49.7 jit_solution(13805550596050749908)
XLA Ops:
  0.0 48.4 %shard_map.118 = f32[1,2048]{1,0:T(1,128)} custom-call(bf16[64,128]{1,0:T(8,128)(2,1)} %bitcast.6, bf16[256,512]{1,0:T(8,128)(2,1)} %table_hbm.1, s32[1,2048]{1,0:T(1,128)} %bitcast.7, s32[64]{0:T(128)} %order_ref.1, s32[1,2048]{1,0:T(1,128)} %bitcast.8, s32[1,2048]{1,0:T(1,128)} %bitcast.9, bf16[256,2048]{1,0:T(8,128)(2,1)} %w_user_hbm.1, ...), custom_call_target="tpu_custom_call" | custom-call | flops 6442450944 | bytes 8388608 | tf_op jit(solution)/shard_map/pallas_call | solution.py:362
  48.4 1.3 %copy.14 = f32[2048]{0:T(1024)} copy(f32[2048]{0:T(1024)} %bitcast.5) | data formatting | bytes 16384

commit v3 on v2

--- a/solution.py
+++ b/solution.py
@@ -25,16 +25,16 @@
     dims,
     users_hbm,
     table_hbm,
-    seg_ref,
+    seg_hbm,
     order_ref,
-    shard_ref,
-    offset_ref,
+    shard_hbm,
+    offset_hbm,
     w_user_hbm,
-    w_dots_ref,
-    w_gram_ref,
+    w_dots_hbm,
+    w_gram_hbm,
     w_item_hbm,
-    bias_ref,
-    w_out_ref,
+    bias_hbm,
+    w_out_hbm,
     out_ref,
     buf,
     xt,
@@ -49,6 +49,13 @@
     wout_b,
     rid,
     req,
+    seg_ref,
+    shard_ref,
+    offset_ref,
+    w_dots_ref,
+    w_gram_ref,
+    bias_ref,
+    w_out_ref,
     load_sem,
     send_sem,
     recv_sem,
@@ -92,6 +99,21 @@
     get_user = pltpu.make_async_copy(w_user_hbm, w_user, load_sem.at[2 * nif + 1])
     get_item.start()
     get_user.start()
+    small = []
+    for k, (source, target) in enumerate(
+        (
+            (seg_hbm, seg_ref),
+            (shard_hbm, shard_ref),
+            (offset_hbm, offset_ref),
+            (w_dots_hbm, w_dots_ref),
+            (w_gram_hbm, w_gram_ref),
+            (bias_hbm, bias_ref),
+            (w_out_hbm, w_out_ref),
+        )
+    ):
+        small.append(pltpu.make_async_copy(source, target, load_sem.at[2 * nif + 2 + k]))
+    for load in small:
+        load.start()
 
     barrier = pltpu.get_barrier_semaphore()
 
@@ -163,11 +185,13 @@
     def finish(c):
         c.wait_send()
 
-    for load in loads:
+    for half in range(2):
+        for load in loads[half * nif : (half + 1) * nif]:
+            load.wait()
+        forward(z, True, half, start)
+
+    for load in small:
         load.wait()
-
-    for half in range(2):
-        forward(z, True, half, start)
 
     xt[...] = jnp.zeros_like(xt)
     gram_t[...] = jnp.zeros_like(gram_t)
@@ -276,7 +300,7 @@
             wut[at, :], gram_t[...].astype(BF16), preferred_element_type=F32
         ).astype(BF16)
 
-    span = 256
+    span = 512
 
     @pl.loop(0, cands // span, unroll=2)
     def _(n):
@@ -362,7 +386,7 @@
     scores = pl.pallas_call(
         functools.partial(kernel, dims),
         out_shape=jax.ShapeDtypeStruct((1, cands), F32),
-        in_specs=[hbm, hbm, vmem, smem, vmem, vmem, hbm, vmem, vmem, hbm, vmem, vmem],
+        in_specs=[hbm] * 3 + [smem] + [hbm] * 8,
         out_specs=vmem,
         scratch_shapes=[
             pltpu.VMEM((num, nif, slot_rows, width), BF16),
@@ -378,7 +402,14 @@
             pltpu.VMEM((hidden, 128), F32),
             pltpu.VMEM((1, cands), I32),
             pltpu.VMEM((1, cands), I32),
-            pltpu.SemaphoreType.DMA((2 * nif + 2,)),
+            pltpu.VMEM((1, cands), I32),
+            pltpu.VMEM((1, cands), I32),
+            pltpu.VMEM((1, cands), I32),
+            pltpu.VMEM(w_dots.shape, BF16),
+            pltpu.VMEM(w_item_gram.shape, BF16),
+            pltpu.VMEM(bias_one.shape, BF16),
+            pltpu.VMEM(w_out.shape, BF16),
+            pltpu.SemaphoreType.DMA((2 * nif + 9,)),
             pltpu.SemaphoreType.DMA((4, num, 2)),
             pltpu.SemaphoreType.DMA((num, 2)),
         ],

time: 49.9 us -> 49.3 us (0.988)
  Pallas kernels: 48.4 us -> 47.8 us
    pallas_call x1, Pallas kernels: 48.4 us -> 47.8 us  [shards(): pl.pallas_call(functools.partial(kernel, dims), out_shape=jax.ShapeDtypeS...]
where the time goes in v3:
time: 49.3 us; the launch traced here: 49.1 us
  Pallas kernels  47.8 us (97%)
  local copies, waits for them, and re-layouts  1.3 us (3%)
    pallas_call x1, Pallas kernels, shards(): pl.pallas_call(functools.partial(kernel, dims), out_shape=jax.ShapeDtypeS...  47.8 us
    unnamed x1, local copies, waits for them, and re-layouts  1.3 us

profile of v3, /device:TPU:0, one launch (start us, length us, event | category | flops | bytes accessed | tf_op | source)
XLA Modules:
  0.0 49.1 jit_solution(13611943049947532204)
XLA Ops:
  0.0 47.8 %shard_map.118 = f32[1,2048]{1,0:T(1,128)} custom-call(bf16[64,128]{1,0:T(8,128)(2,1)} %bitcast.6, bf16[256,512]{1,0:T(8,128)(2,1)} %table_hbm.1, s32[1,2048]{1,0:T(1,128)} %bitcast.7, s32[64]{0:T(128)} %order_ref.1, s32[1,2048]{1,0:T(1,128)} %bitcast.8, s32[1,2048]{1,0:T(1,128)} %bitcast.9, bf16[256,2048]{1,0:T(8,128)(2,1)} %w_user_hbm.1, ...), custom_call_target="tpu_custom_call" | custom-call | flops 6442450944 | bytes 8388608 | tf_op jit(solution)/shard_map/pallas_call | solution.py:386
  47.8 1.3 %copy.14 = f32[2048]{0:T(1024)} copy(f32[2048]{0:T(1024)} %bitcast.5) | data formatting | bytes 16384
